TPU v7x, 128 devices: a whole 4x4x4 slice. The times are simulated.
128 devices in a mesh: lat: 8 (over x, y_lo), lon: 16 (over y_hi, z, core).
Axes of the slice: x: 4, y: 4 (y_hi: 2, y_lo: 2; y = y_hi * 2 + y_lo), z: 4, core: 2. Of those that a mesh axis runs over, the one named last changes fastest.
Arguments:
- tokens: bfloat16 [192, 384, 512], P('lat', 'lon'), may hold values from -6 to 6
- qkv_fine: bfloat16 [512, 1536], replicated, may hold values from -2 to 2, as said below
- out_fine: bfloat16 [512, 512], replicated, may hold values from -0.25 to 0.25
- merge_fine: bfloat16 [2048, 1024], replicated, may hold values from -0.125 to 0.125
- qkv_mid: bfloat16 [1024, 3072], replicated, may hold values from -2 to 2, as said below
- out_mid: bfloat16 [1024, 1024], replicated, may hold values from -0.1875 to 0.1875
- merge_mid: bfloat16 [4096, 2048], P('lon'), may hold values from -0.09375 to 0.09375
- qkv_coarse: bfloat16 [2048, 6144], P(None, 'lon'), may hold values from -2 to 2, as said below
- out_coarse: bfloat16 [2048, 2048], P('lon'), may hold values from -0.125 to 0.125
- grad_fine: bfloat16 [192, 384, 512], P('lat', 'lon'), may hold values from -6 to 6
- grad_mid: bfloat16 [96, 192, 1024], P('lat', 'lon'), may hold values from -6 to 6
- grad_coarse: bfloat16 [48, 96, 2048], P('lat', 'lon'), may hold values from -6 to 6
Outputs:
- grad_input: bfloat16 [192, 384, 512], P('lat', 'lon')
- coarse: bfloat16 [48, 96, 2048], P('lat', 'lon')
Inputs may be any that keep to these rules, and one draw needn't show every extreme that they name: `qkv_fine`: head-major columns: each head's query, key and value blocks of 64 columns lie side by side. `qkv_mid`: head-major columns as for qkv_fine. `qkv_coarse`: head-major columns as for qkv_fine.
All inputs are finite; a program needn't handle non-finite values.
Results may differ from a plain program's by a relative error of at most 0.029.
Values may be sent and summed in bfloat16 or wider, within the bound.
A program may use at most 128 MiB of HBM per device.

v0:
```python
from types import SimpleNamespace

import jax
import jax.numpy as jnp
import numpy as np
from jax import lax
from jax.experimental import pallas as pl
from jax.experimental.pallas import tpu as pltpu
from jax.sharding import PartitionSpec as P

HD = 64
WH = 6
WW = 12
WP = 80
KP = 48
EPS = 1e-05
LAT = 8
LON = 16
bf16 = jnp.bfloat16
f32 = jnp.float32
MESH = pl.DeviceIdType.MESH


def window_order(cols):
    across = cols // WW

    def index(r, c):
        return ((r // WH) * across + c // WW) * WP + (r % WH) * WW + c % WW

    return index


def raster(stride):
    return lambda r, c: r * stride + c


def fold_order(inner, stride):
    def index(r, c):
        return ((c % 2) * 2 + r % 2) * stride + inner(r // 2, c // 2)

    return index


def shift_maps(size, src, n_src, dst, n_dst):
    dr, dc = WH // 2, WW // 2
    up = -(-(size - dr) * dc // 32) * 32
    down = -(-max(dr * (size - dc), 0) // 32) * 32
    corner = 32
    parts = [(0, up, 0, 1), (up, down, 1, 0), (up + down, corner, 1, 1)]
    total = up + down + corner
    own = np.zeros((n_dst, n_src), np.float32)
    halo = np.zeros((n_dst, total), np.float32)
    pack = np.zeros((total, n_src), np.float32)
    for r in range(size):
        for c in range(size):
            to = dst(r, c)
            if r >= dr and c >= dc:
                own[to, src(r - dr, c - dc)] = 1
                continue
            if r >= dr:
                slot = (r - dr) * dc + c
            elif c >= dc:
                slot = up + r * (size - dc) + c - dc
            else:
                slot = up + down + r * dc + c
            halo[to, slot] = 1
            pack[slot, src((r - dr) % size, (c - dc) % size)] = 1
    return own, halo, pack, [part for part in parts if part[1]]


def window_bias(stride, rows, groups):
    token = np.arange(rows)
    real = token % stride < groups * 2
    upper = token % stride < groups
    allowed = np.broadcast_to(real[None, :], (rows, rows))
    split = allowed & (upper[:, None] == upper[None, :])
    both = np.stack([allowed, split])
    both = np.concatenate([both, both], 1)
    return np.where(both, 0.0, -1e30).astype(np.float32)


FINE = shift_maps(24, raster(24), 576, window_order(24), 640)
FOLD = shift_maps(24, window_order(24), 640, fold_order(window_order(12), 160), 640)
MID = shift_maps(12, raster(16), 192, window_order(12), 160)
FOLDC = shift_maps(12, window_order(12), 160, fold_order(raster(6), KP), 4 * KP)
COARSE = shift_maps(6, raster(16), 96, raster(6), KP)
BIAS = window_bias(WP, WP, 36)
BIASC = window_bias(KP, 2 * KP, 18)

SQUEEZE = np.zeros((144, 4 * KP), np.float32)
for k in range(4):
    SQUEEZE[k * 36 : (k + 1) * 36, k * KP : k * KP + 36] = np.eye(36)
TOP = 80
FINE_BAND = np.ascontiguousarray(FINE[0][160:320, 144 - TOP : 304 - TOP])
FINE_BAND_BACK = np.ascontiguousarray(FINE[0][160:480, 144:288].T)
CONSTANTS = dict(
    fine_own=FINE_BAND, fine_halo=FINE[1], fine_pack=FINE[2],
    fine_own_t=FINE_BAND_BACK, fine_halo_t=FINE[1].T, fine_pack_t=FINE[2].T,
    fold_own=FOLD[0], fold_halo=FOLD[1], fold_pack=FOLD[2], fold_halo_t=FOLD[1].T, fold_pack_t=FOLD[2].T,
    mid_own=MID[0], mid_halo=MID[1], mid_pack=MID[2],
    foldc_own=FOLDC[0], foldc_halo=FOLDC[1], foldc_pack=FOLDC[2],
    foldc_own_t=FOLDC[0].T, foldc_halo_t=FOLDC[1].T, foldc_pack_t=FOLDC[2].T,
    squeeze=SQUEEZE, squeeze_t=SQUEEZE.T,
    coarse_halo=COARSE[1], coarse_pack=COARSE[2], coarse_halo_t=COARSE[1].T, coarse_pack_t=COARSE[2].T,
)

LOADED = (
    tuple(dict(tokens=1, fine_pack=1, fine_own=1, fine_halo=1)),
    tuple(dict(
        qkv_f=1, g_coarse=1, coarse_pack=1, g_mid=1, mid_pack=1, g_fine=1, bias=1, out_f=1, fold_pack=1, fold_own=1, fold_halo=1,
    )),
    tuple(dict(
        mrg_f=1, coarse_halo=1, squeeze=1, squeeze_t=1, qkv_m=1, out_m=1, foldc_pack=1, foldc_own=1, foldc_halo=1, biasc=1,
        mid_own=1, mid_halo=1, foldc_halo_t=1, foldc_own_t=1, foldc_pack_t=1, fold_halo_t=1, fold_pack_t=1,
        fine_halo_t=1, fine_own_t=1, fine_pack_t=1, coarse_halo_t=1, coarse_pack_t=1,
    )),
)
ALL_LOADED = [name for group in LOADED for name in group]


def nn(a, b):
    return jnp.dot(a, b, preferred_element_type=f32)


def nt(a, b):
    return lax.dot_general(a, b, (((1,), (1,)), ((), ())), preferred_element_type=f32)


def tn(a, b):
    return lax.dot_general(a, b, (((0,), (0,)), ((), ())), preferred_element_type=f32)


def norm_rows(x):
    centred = x - jnp.mean(x, axis=-1, keepdims=True)
    scale = lax.rsqrt(jnp.mean(centred * centred, axis=-1, keepdims=True) + EPS)
    return centred * scale, scale


def norm_back(d, h, scale):
    d = d.astype(bf16).astype(f32)
    h = h.astype(f32)
    return scale * (d - jnp.mean(d, axis=-1, keepdims=True) - h * jnp.mean(d * h, axis=-1, keepdims=True))


def norm_split(parts):
    size = sum(p.shape[-1] for p in parts)
    average = sum(jnp.sum(p, axis=-1, keepdims=True) for p in parts) / size
    parts = [p - average for p in parts]
    scale = lax.rsqrt(sum(jnp.sum(p * p, axis=-1, keepdims=True) for p in parts) / size + EPS)
    return [p * scale for p in parts], scale


def norm_back_split(ds, hs, scale):
    size = sum(d.shape[-1] for d in ds)
    ds = [d.astype(bf16).astype(f32) for d in ds]
    hs = [h.astype(f32) for h in hs]
    mean_d = sum(jnp.sum(d, axis=-1, keepdims=True) for d in ds) / size
    mean_dh = sum(jnp.sum(d * h, axis=-1, keepdims=True) for d, h in zip(ds, hs)) / size
    return [scale * (d - mean_d - h * mean_dh) for d, h in zip(ds, hs)]


def aligned(start, size, multiple):
    return pl.ds(pl.multiple_of(start, multiple), size)


def project_qkv(h, weight, tr, trr, rows, pairs, step):
    @pl.loop(0, rows // step)
    def _(i):
        part = aligned(i * step, step, 16)

        @pl.loop(0, pairs)
        def _(p):
            wide = nn(h[part, :], weight(p))
            tr[part, aligned(p * 384, 384, 128)] = wide.astype(bf16)
            ra, rb, rc = (pltpu.roll(wide[:, k * 128 : (k + 1) * 128], 64, 1) for k in range(3))
            low = lax.broadcasted_iota(jnp.int32, (1, 128), 1) < 64
            trr[part, aligned(p * 256, 128, 128)] = jnp.where(low, ra, rc).astype(bf16)
            trr[part, aligned(p * 256 + 128, 128, 128)] = jnp.where(low, rb, ra).astype(bf16)


def halves():
    lane = lax.broadcasted_iota(jnp.int32, (1, 128), 1)
    low = lane < 64
    one = jnp.where(low, 1.0, 0.0)
    return low, one.astype(bf16), (1.0 - one).astype(bf16)


def attend(tr, trr, ps, mix, bias, pairs, windows, wp, split, unroll, part=0, parts=1):
    steps = pairs * windows // unroll // parts

    @pl.loop(part * steps, (part + 1) * steps)
    def _(step):
        low, mlo, mhi = halves()
        for u in range(unroll):
            item = step * unroll + u
            w, p = lax.div(item, pairs), lax.rem(item, pairs)
            part = aligned(w * wp, wp, 16)
            a, b, c = (tr[part, aligned(p * 384 + k * 128, 128, 128)] for k in range(3))
            k2 = trr[part, aligned(p * 256, 128, 128)]
            eighth = jnp.asarray(HD**-0.5, bf16)
            q2 = jnp.concatenate([a * (mlo * eighth), b * (mhi * eighth)], 0)
            scores = nt(q2, k2) + bias[split(w)]
            e = jnp.exp(scores - jnp.max(scores, axis=-1, keepdims=True))
            weights = (e / jnp.sum(e, axis=-1, keepdims=True)).astype(bf16)
            ps[item] = weights
            mixed = jnp.where(low, nn(weights[:wp], b), nn(weights[wp:], c))
            mix[part, aligned(p * 128, 128, 128)] = mixed.astype(bf16)


def attend_back(tr, trr, ps, dmix, pairs, windows, wp, unroll):
    @pl.loop(0, pairs * windows // unroll)
    def _(step):
        low, mlo, mhi = halves()
        for u in range(unroll):
            item = step * unroll + u
            w, p = lax.div(item, pairs), lax.rem(item, pairs)
            part = aligned(w * wp, wp, 16)
            places = [(part, aligned(p * 384 + k * 128, 128, 128)) for k in range(3)]
            b, c = tr[places[1]], tr[places[2]]
            k2, q2 = (trr[part, aligned(p * 256 + k * 128, 128, 128)] for k in range(2))
            do = dmix[part, aligned(p * 128, 128, 128)]
            weights = ps[item]
            outs = []
            for half, mask, values in ((0, mlo, b), (1, mhi, c)):
                wt = weights[half * wp : (half + 1) * wp]
                wide = wt.astype(f32)
                dw = nt(do * mask, values)
                ds = wide * (dw - jnp.sum(wide * dw, axis=-1, keepdims=True)) * HD**-0.5
                outs.append((wt, ds.astype(bf16)))
            (w0, ds0), (w1, ds1) = outs
            tr[places[0]] = jnp.where(low, nn(ds0, k2), tn(ds0, q2)).astype(bf16)
            tr[places[1]] = jnp.where(low, tn(w0, do), nn(ds1, k2)).astype(bf16)
            tr[places[2]] = jnp.where(low, tn(ds1, q2), tn(w1, do)).astype(bf16)


def tiles(rows, step, cols, width, body):
    @pl.loop(0, rows // step)
    def _(i):
        part = aligned(i * step, step, 16)

        @pl.loop(0, cols // width)
        def _(j):
            body(part, aligned(j * width, width, 128))


VMEM_SCRATCH = dict(
    xf=((640, 512), bf16), hf=((640, 512), bf16), sf=((640, 1), f32), trf=((640, 1536), bf16),
    trrf=((640, 1024), bf16), psf=((32, 2 * WP, WP), bf16), mixf=((640, 512), bf16), yf=((640, 512), bf16),
    wide=((640, 512), f32),
    ff=((160, 2048), bf16), sff=((160, 1), f32),
    xm=((160, 1024), bf16), hm=((160, 1024), bf16), sm=((160, 1), f32), trm=((160, 3072), bf16),
    trrm=((160, 2048), bf16), psm=((16, 2 * WP, WP), bf16), mixm=((160, 1024), bf16), ym=((160, 1024), bf16),
    fc=((KP, 4096), bf16), sfc=((KP, 1), f32), fcs=((4, KP, 1024), bf16), fcr=((4, KP, 1024), bf16),
    pms=((4, 144, 512), bf16), pmr=((4, 144, 512), bf16), dmo=((144, 512), bf16), dms=((4, 144, 512), bf16), stage=((4, KP, 2048), bf16),
    dsr=((4, KP, 1024), bf16), dfc=((4 * KP, 1024), bf16),
    gm=((192, 1024), bf16), gc=((96, 2048), bf16),
    xc=((KP, 2048), bf16), hc=((KP, 2048), bf16), sc=((KP, 1), f32), hcs=((144, 512), bf16), hcr=((4, 144, 512), bf16),
    ac=((KP, 2048), bf16), acs=((144, 512), bf16), acr=((4, 144, 512), bf16),
    trc=((4 * KP, 1536), bf16), trrc=((4 * KP, 1024), bf16), psc=((8, 4 * KP, 2 * KP), bf16),
    mixc=((4 * KP, 512), bf16), dmixc=((4 * KP, 512), bf16),
    dhs=((4, 144, 512), bf16), dhr=((4, 144, 512), bf16), pos=((4, 144, 512), bf16), por=((4, 144, 512), bf16),
    yc=((KP, 2048), bf16),
    wm=((4, 256, 2048), bf16), wq=((4, 2048, 384), bf16), wo=((4, 128, 2048), bf16),
)
EXCHANGES = dict(
    tok=(FINE, 512, 1), gf=(FINE, 512, 1), gm=(MID, 1024, 1), gc=(COARSE, 2048, 1), fold=(FOLD, 512, 1), foldc=(FOLDC, 1024, 1),
    foldc_b=(FOLDC, 1024, -1), fold_b=(FOLD, 512, -1), fine_b=(FINE, 512, -1), coarse_b=(COARSE, 2048, -1),
)
SENT_FROM = dict(fold="tok", fold_b="tok", fine_b="tok", foldc_b="foldc", coarse_b="gc")
N_LOCAL = len(ALL_LOADED) + 7
N_REMOTE = 96


class Lazy:
    def __init__(self, make):
        self.make = make

    def __getattr__(self, name):
        value = self.make(name)
        setattr(self, name, value)
        return value


def build(shapes):
    scratch = dict(VMEM_SCRATCH)
    loaded = {name: shapes[name] for name in ALL_LOADED}
    for name in ("tokens", "g_fine"):
        loaded[name] = ((TOP + 576, 512), bf16)
    sends, receives = {}, {}
    for name, (maps, width, _) in EXCHANGES.items():
        receives[name] = ((maps[1].shape[1], width), bf16)
        if name not in SENT_FROM:
            sends[name] = receives[name]

    def kernel(*refs):
        refs = list(refs)

        def take(names):
            return {name: refs.pop(0) for name in names}

        hbm = take(shapes)
        grad_ref, coarse_ref = refs.pop(0), refs.pop(0)
        v = SimpleNamespace(**take(scratch))
        vm, send_buf, recv_buf = take(loaded), take(sends), take(receives)
        local_sem, send_sem, recv_sem = refs

        lat, lon = lax.axis_index("lat"), lax.axis_index("lon")
        y, z, core = lax.div(lon, 8), lax.rem(lax.div(lon, 2), 4), lax.rem(lon, 2)

        def near(dlat, dlon):
            return (lax.rem(lat + dlat + LAT, LAT), lax.rem(lon + dlon + LON, LON))

        def at(yy, zz, cc):
            return (lat, yy * 8 + zz * 2 + cc)

        def turn(k):
            return lax.rem(z + k, 4)

        loads = {}
        for i, name in enumerate(ALL_LOADED):
            dest = vm[name].at[pl.ds(TOP, 576)] if name in ("tokens", "g_fine") else vm[name]
            loads[name] = pltpu.make_async_copy(hbm[name], dest, local_sem.at[i])

        def start_loads(group):
            for name in group:
                loads[name].start()

        start_loads(LOADED[0])

        def wait_load(name):
            loads[name].wait()
            return vm[name]

        got = Lazy(wait_load)

        own_slot = y * 2 + core
        own_loads = []
        for i, name in enumerate(("wm", "wq", "wo")):
            copy = pltpu.make_async_copy(hbm[name], getattr(v, name).at[own_slot], local_sem.at[len(ALL_LOADED) + i])
            own_loads.append(copy)

        barrier = pltpu.get_barrier_semaphore()
        others = [near(1, 0), near(-1, 0), near(1, 1), near(-1, -1)]
        others += [(lat + 1 - 2 * lax.rem(lat, 2), lax.rem(lon + 8, LON))]
        others += [(lat, y * 8 + lax.rem(lax.rem(lon, 8) + k, 8)) for k in range(1, 8)]
        for device in others:
            pl.semaphore_signal(barrier, inc=1, device_id=device, device_id_type=MESH)
        place = lax.rem(lon, 8)

        @pl.when(place == 7)
        def _():
            pl.semaphore_signal(barrier, inc=1, device_id=near(0, 1), device_id_type=MESH)

        @pl.when(place == 0)
        def _():
            pl.semaphore_signal(barrier, inc=1, device_id=near(0, -1), device_id_type=MESH)

        edge = jnp.where((place == 7) | (place == 0), 1, 0)
        pl.semaphore_wait(barrier, len(others) + edge)

        counter = [0]

        def sems(n):
            counter[0] += n
            assert counter[0] <= N_REMOTE
            return counter[0] - n

        def remote(src, dst, send, recv, device):
            return pltpu.make_async_remote_copy(
                src_ref=src, dst_ref=dst, send_sem=send_sem.at[send], recv_sem=recv_sem.at[recv],
                device_id=device, device_id_type=MESH,
            )

        pending = []

        def sender(name):
            return send_buf[SENT_FROM.get(name, name)]

        def finish(copies):
            for copy in copies:
                copy.wait()

        def sent(copies):
            for copy in copies:
                copy.wait_send()

        def shift(name):
            maps, _, sign = EXCHANGES[name]
            base = sems(3)
            copies = []
            for k, (start, size, dlat, dlon) in enumerate(maps[3]):
                part = pl.ds(start, size)
                copies.append(
                    remote(sender(name).at[part], recv_buf[name].at[part], base + k, base + k, near(sign * dlat, sign * dlon))
                )
            for copy in copies:
                copy.start()
            return copies

        def received(copies):
            for copy in copies:
                copy.wait_recv()

        sibling = at(y, z, 1 - core)
        partner_slot = (1 - y) * 2 + core
        y_low = lax.rem(lat, 2)
        beside = lat + 1 - 2 * y_low

        def weight_piece(name, start, size):
            base = sems(2)
            dest = getattr(v, name)
            half = hbm[name].shape[0] // 2
            mine = aligned(y_low * half + start, size, 16)
            other = aligned((1 - y_low) * half + start, size, 16)
            there = dest.at[partner_slot, other]
            return (
                remote(hbm[name].at[mine], dest.at[own_slot, mine], base, base, (beside, lax.rem(lon + 8, LON))),
                remote(there, there, base + 1, base + 1, (beside, lon)),
            )

        def core_copies(name):
            base = sems(2)
            dest = getattr(v, name)
            there = dest.at[partner_slot]
            return (
                remote(hbm[name], dest.at[own_slot], base, base, sibling),
                remote(there, there, base + 1, base + 1, sibling),
            )

        pieces = dict(
            wm=[weight_piece("wm", 0, 128)],
            wq=[weight_piece("wq", 0, 640), weight_piece("wq", 640, 384)],
            wo=[weight_piece("wo", 0, 64)],
        )
        between_cores = {name: core_copies(name) for name in pieces}

        def cross_weights(name, i):
            pieces[name][i][0].start()

        def relay_weights(name, i):
            pieces[name][i][0].wait_recv()
            pieces[name][i][1].start()

        def pass_weights(name):
            for piece in pieces[name]:
                piece[1].wait_recv()
            between_cores[name][1].start()

        def weights_ready(name):
            for copy in between_cores[name]:
                copy.wait_recv()
                pending.append(copy)
            for piece in pieces[name]:
                pending.extend(piece)

        def pack(name, source, matrix):
            sender(name)[...] = nn(matrix[...], source).astype(bf16)

        tokens = got.tokens
        pack("tok", tokens[TOP:, :], got.fine_pack)
        shift_tok = shift("tok")
        start_loads(LOADED[1])
        tokens[0:TOP, :] = jnp.zeros((TOP, 512), bf16)
        vm["g_fine"][0:TOP, :] = jnp.zeros((TOP, 512), bf16)
        v.gm[...] = jnp.zeros_like(v.gm)
        v.gc[...] = jnp.zeros_like(v.gc)
        fine_own, fine_halo, qkv_f = got.fine_own, got.fine_halo, got.qkv_f

        def placed(part, source, name, own, halo):
            return nn(own[part, :], source[...]) + nn(halo[part, :], recv_buf[name][...])

        def placed_fine(i, source, name):
            return nn(fine_own[...], source[aligned(i * 144, 160, 16), :]) + nn(
                fine_halo[aligned(i * 160, 160, 16), :], recv_buf[name][...]
            )

        received(shift_tok)
        cross_weights("wm", 0)

        @pl.loop(0, 4)
        def _(i):
            part = aligned(i * 160, 160, 16)
            x = placed_fine(i, tokens, "tok")
            v.xf[part, :] = x.astype(bf16)
            h, scale = norm_rows(x)
            v.hf[part, :] = h.astype(bf16)
            v.sf[part, :] = scale

        start_loads(LOADED[2])
        for copy in own_loads:
            copy.start()
        for name in pieces:
            between_cores[name][0].start()
        project_qkv(v.hf, lambda p: qkv_f[:, aligned(p * 384, 384, 128)], v.trf, v.trrf, 640, 4, 320)
        first = lat == 0
        bias, out_f = got.bias, got.out_f
        for part in range(2):
            if part == 1:
                relay_weights("wm", 0)
                for r in range(6):
                    v.gc[16 * r : 16 * r + 6, :] = got.g_coarse[r]
                for r in range(12):
                    v.gm[16 * r : 16 * r + 12, :] = got.g_mid[r]
                pack("gc", v.gc[...], got.coarse_pack)
                shift_gc = shift("gc")
                pack("gf", got.g_fine[TOP:, :], got.fine_pack)
                shift_gf = shift("gf")
                pack("gm", v.gm[...], got.mid_pack)
                shift_gm = shift("gm")
                cross_weights("wq", 0)
            attend(v.trf, v.trrf, v.psf, v.mixf, bias, 4, 8, WP, lambda w: jnp.where(first & (w < 2), 1, 0), 4, part, 2)

        def out_fine(part, cols):
            v.yf[part, cols] = (nn(v.mixf[part, :], out_f[:, cols]) + v.xf[part, cols].astype(f32)).astype(bf16)

        tiles(640, 320, 512, 256, out_fine)

        sent(shift_tok)
        pack("fold", v.yf[...], got.fold_pack)
        shift_fold = shift("fold")
        fold_own, fold_halo, mrg_f = got.fold_own, got.fold_halo, got.mrg_f
        slot = lax.rem(z, 2) * 2 + core
        wide_group = lax.div(z, 2)

        def squeeze(x, dest):
            stacked = jnp.concatenate([x[:, k * 512 : (k + 1) * 512] for k in range(4)], 0)
            dest[...] = nn(got.squeeze[...], stacked).astype(bf16)

        def spread(packed):
            stacked = nn(got.squeeze_t[...], packed.astype(bf16))
            return [stacked[k * KP : (k + 1) * KP] for k in range(4)]

        def spread_all(packed):
            for s in range(4):
                for k, part in enumerate(spread(packed[s])):
                    v.stage[s, :, k * 512 : (k + 1) * 512] = part.astype(bf16)

        def total_of(packed):
            return jnp.concatenate(spread(sum(packed[k].astype(f32) for k in range(4))), 1)

        def to_group(source, dest):
            send, recv = sems(4), sems(4)
            for k in range(1, 4):
                copy = remote(source, dest.at[slot], send + k, recv + slot, at(y, turn(k), wide_group))
                copy.start()
                pending.append(copy)
            across = remote(source, dest.at[slot], send, recv + slot, sibling)

            @pl.when(core == wide_group)
            def _():
                dest[slot] = source[...]

            @pl.when(core != wide_group)
            def _():
                across.start()
                across.wait_send()

            return source, dest, send, recv

        def is_own(s):
            return (z == core * 2 + s // 2) & (core == s % 2)

        def from_group(handle):
            source, dest, send, recv = handle
            for s in range(4):

                @pl.when(jnp.logical_not(is_own(s)))
                def _(s=s):
                    remote(source, dest.at[s], send, recv + s, sibling).wait_recv()

        def to_owners(source, dest):
            send, recv = sems(4), sems(4)
            for s in range(4):
                copy = remote(source.at[s], dest.at[z], send + s, recv + z, at(y, core * 2 + s // 2, s % 2))

                @pl.when(is_own(s))
                def _(s=s):
                    dest[z] = source[s]

                @pl.when(jnp.logical_not(is_own(s)))
                def _(copy=copy):
                    copy.start()

            return source, dest, send, recv

        def from_members(handle):
            source, dest, send, recv = handle
            for k in range(4):

                @pl.when(jnp.logical_not((z == k) & (core == wide_group)))
                def _(k=k):
                    remote(source.at[0], dest.at[k], send, recv + k, sibling).wait_recv()

            for s in range(4):

                @pl.when(jnp.logical_not(is_own(s)))
                def _(s=s):
                    remote(source.at[s], dest.at[0], send + s, recv, sibling).wait_send()

        def around(pick, dest, own):
            base = sems(4)
            copies = []
            for k in range(1, 4):
                copy = remote(pick(k), dest.at[z], base + k, base + k, at(y, turn(k), core))
                copy.start()
                copies.append(copy)
            dest[z] = own
            return copies

        received(shift_fold)

        quads = [placed(slice(k * 160, (k + 1) * 160), v.yf, "fold", fold_own, fold_halo) for k in range(4)]
        normed, scale = norm_split(quads)
        for k in range(4):
            v.ff[:, k * 512 : (k + 1) * 512] = normed[k].astype(bf16)
        v.sff[...] = scale
        relay_weights("wq", 0)
        cross_weights("wq", 1)
        finish(shift_gf)
        finish(shift_gc)
        v.ac[...] = nn(got.coarse_halo[...], recv_buf["gc"][...]).astype(bf16)
        squeeze(v.ac[...], v.acs)
        adjoint = to_group(v.acs, v.acr)

        @pl.loop(0, 4)
        def _(i):
            part = aligned(i * 160, 160, 16)
            v.yf[part, :] = placed_fine(i, got.g_fine, "gf").astype(bf16)

        def merge_fine(part, cols):
            v.xm[part, cols] = nn(v.ff[part, :], mrg_f[:, cols]).astype(bf16)

        tiles(160, 160, 1024, 256, merge_fine)

        qkv_m, out_m = got.qkv_m, got.out_m
        h, scale = norm_rows(v.xm[...].astype(f32))
        v.hm[...] = h.astype(bf16)
        v.sm[...] = scale
        project_qkv(v.hm, lambda p: qkv_m[:, aligned(p * 384, 384, 128)], v.trm, v.trrm, 160, 8, 160)
        attend(v.trm, v.trrm, v.psm, v.mixm, bias, 8, 2, WP, lambda w: jnp.where(first & (w < 1), 1, 0), 4)

        pass_weights("wm")

        def out_mid(part, cols):
            v.ym[part, cols] = (nn(v.mixm[part, :], out_m[:, cols]) + v.xm[part, cols].astype(f32)).astype(bf16)

        tiles(160, 160, 1024, 256, out_mid)

        pack("foldc", v.ym[...], got.foldc_pack)
        shift_foldc = shift("foldc")
        for copy in own_loads:
            copy.wait()
        weights_ready("wm")
        foldc_own, foldc_halo = got.foldc_own, got.foldc_halo
        received(shift_foldc)
        relay_weights("wq", 1)
        cross_weights("wo", 0)
        folded = placed(slice(None), v.ym, "foldc", foldc_own, foldc_halo)
        quads = [folded[k * KP : (k + 1) * KP] for k in range(4)]
        normed, scale = norm_split(quads)
        v.sfc[...] = scale
        for k in range(4):
            h = normed[k].astype(bf16)
            v.fc[:, k * 1024 : (k + 1) * 1024] = h
            for j in range(2):
                block = 2 * k + j
                v.fcs[block % 4, :, (block // 4) * 512 : (block // 4 + 1) * 512] = h[:, j * 512 : (j + 1) * 512]
        copies = around(lambda k: v.fcs.at[turn(k)], v.fcr, v.fcs[z])
        finish(copies)
        gathered = v.fcr[...].reshape(4 * KP, 1024)

        @pl.loop(0, 8)
        def _(j):
            cols = aligned(j * 256, 256, 128)
            total = nn(gathered[:, 0:256], v.wm[0, :, cols])
            for s in range(1, 4):
                total += nn(gathered[:, s * 256 : (s + 1) * 256], v.wm[s, :, cols])
            v.stage[:, :, cols] = total.astype(bf16).reshape(4, KP, 256)

        for k in range(4):
            squeeze(v.stage[k], v.pms.at[k])
        copies = around(lambda k: v.pms.at[turn(k)], v.pmr, v.pms[z])
        relay_weights("wo", 0)
        pass_weights("wq")
        finish(copies)
        x = total_of(v.pmr).astype(bf16)
        v.xc[...] = x
        h, scale = norm_rows(x.astype(f32))
        v.hc[...] = h.astype(bf16)
        v.sc[...] = scale

        squeeze(v.hc[...], v.hcs)
        forward = to_group(v.hcs, v.hcr)
        biasc = got.biasc
        weights_ready("wq")
        from_group(forward)
        spread_all(v.hcr)
        pass_weights("wo")
        project_qkv(v.stage.reshape(4 * KP, 2048), lambda p: v.wq[p], v.trc, v.trrc, 4 * KP, 4, 4 * KP)
        attend(v.trc, v.trrc, v.psc, v.mixc, biasc, 4, 2, 2 * KP, lambda w: jnp.where(first, 1, 0), 4)
        from_group(adjoint)
        weights_ready("wo")
        spread_all(v.acr)
        for p in range(4):
            v.dmixc[:, p * 128 : (p + 1) * 128] = nt(v.stage[...].reshape(4 * KP, 2048), v.wo[p]).astype(bf16)
        attend_back(v.trc, v.trrc, v.psc, v.dmixc, 4, 2, 2 * KP, 4)

        @pl.loop(0, 8)
        def _(j):
            rows = aligned(j * 256, 256, 128)
            total = nt(v.trc[:, 0:384], v.wq[0, rows, :])
            for s in range(1, 4):
                total += nt(v.trc[:, s * 384 : (s + 1) * 384], v.wq[s, rows, :])
            v.stage[:, :, rows] = total.astype(bf16).reshape(4, KP, 256)

        for k in range(4):
            squeeze(v.stage[k], v.dhs.at[k])
        backward = to_owners(v.dhs, v.dhr)

        @pl.loop(0, 8)
        def _(j):
            cols = aligned(j * 256, 256, 128)
            total = nn(v.mixc[:, 0:128], v.wo[0, :, cols])
            for s in range(1, 4):
                total += nn(v.mixc[:, s * 128 : (s + 1) * 128], v.wo[s, :, cols])
            v.stage[:, :, cols] = total.astype(bf16).reshape(4, KP, 256)

        for k in range(4):
            squeeze(v.stage[k], v.pos.at[k])
        from_members(backward)
        d = total_of(v.dhr)
        d = norm_back(d, v.hc[...], v.sc[...])
        d = (d.astype(bf16).astype(f32) + v.ac[...].astype(f32)).astype(bf16)
        squeeze(d, v.dmo)

        copies = around(lambda k: v.dmo, v.dms, v.dmo[...])
        finish(copies)
        spread_all(v.dms)
        gathered_d = v.stage[...].reshape(4 * KP, 2048)
        for s in range(4):
            block = nt(gathered_d, v.wm[s]).astype(bf16)
            v.fcs[:, :, s * 256 : (s + 1) * 256] = block.reshape(4, KP, 256)
        copies = around(lambda k: v.fcs.at[turn(k)], v.dsr, v.fcs[z])
        outward = to_owners(v.pos, v.por)
        finish(copies)

        ds = []
        hs = []
        for b in range(8):
            ds.append(v.dsr[b % 4, :, (b // 4) * 512 : (b // 4 + 1) * 512])
            hs.append(v.fc[:, b * 512 : (b + 1) * 512])
        for b, d in enumerate(norm_back_split(ds, hs, v.sfc[...])):
            k = b // 2
            v.dfc[k * KP : (k + 1) * KP, (b % 2) * 512 : (b % 2 + 1) * 512] = d.astype(bf16)
        sent(shift_foldc)
        pack("foldc_b", v.dfc[...], got.foldc_halo_t)
        copies = shift("foldc_b")
        foldc_own_t, foldc_pack_t = got.foldc_own_t, got.foldc_pack_t
        finish(shift_gm)
        adjoint_mid = placed(slice(None), v.gm, "gm", got.mid_own, got.mid_halo).astype(bf16).astype(f32)
        finish(copies)
        d = placed(slice(None), v.dfc, "foldc_b", foldc_own_t, foldc_pack_t)
        v.ym[...] = (adjoint_mid + d.astype(bf16).astype(f32)).astype(bf16)

        def dmix_mid(part, cols):
            v.mixm[part, cols] = nt(v.ym[part, :], out_m[cols, :]).astype(bf16)

        tiles(160, 160, 1024, 256, dmix_mid)
        attend_back(v.trm, v.trrm, v.psm, v.mixm, 8, 2, WP, 4)

        from_members(outward)
        total = total_of(v.por)
        v.yc[...] = (v.xc[...].astype(f32) + total).astype(bf16)
        pack("coarse_b", v.yc[...], got.coarse_halo_t)
        shift_out = shift("coarse_b")

        def to_wide(left, weight, blocks):
            @pl.loop(0, 2 * blocks)
            def _(j):
                v.wide[aligned(lax.div(j, 2) * 160, 160, 16), aligned(lax.rem(j, 2) * 256, 256, 128)] = nt(
                    left[...], weight[aligned(j * 256, 256, 128), :]
                )

        def wide_back(blocks, h, scale):
            ds = [v.wide[k * 160 : (k + 1) * 160, :] for k in range(blocks)]
            hs = [h[:, k * 512 : (k + 1) * 512] for k in range(blocks)]
            return [d.astype(bf16) for d in norm_back_split(ds, hs, scale[...])]

        to_wide(v.trm, qkv_m, 2)
        for k, d in enumerate(wide_back(2, v.hm, v.sm)):
            cols = slice(k * 512, (k + 1) * 512)
            v.xm[:, cols] = (d.astype(f32) + v.ym[:, cols].astype(f32)).astype(bf16)

        to_wide(v.xm, mrg_f, 4)
        for k, d in enumerate(wide_back(4, v.ff, v.sff)):
            v.mixf[k * 160 : (k + 1) * 160, :] = d
        sent(shift_fold)
        pack("fold_b", v.mixf[...], got.fold_halo_t)
        copies = shift("fold_b")
        fold_pack_t = got.fold_pack_t
        finish(copies)

        @pl.loop(0, 5)
        def _(i):
            part = aligned(i * 128, 128, 128)
            d = tn(fold_own[:, part], v.mixf[...]) + nn(fold_pack_t[part, :], recv_buf["fold_b"][...])
            v.yf[part, :] = (v.yf[part, :].astype(f32) + d.astype(bf16).astype(f32)).astype(bf16)

        def dmix_fine(part, cols):
            v.mixf[part, cols] = nt(v.yf[part, :], out_f[cols, :]).astype(bf16)

        tiles(640, 320, 512, 256, dmix_fine)
        attend_back(v.trf, v.trrf, v.psf, v.mixf, 4, 8, WP, 4)

        def dh_fine(part, cols):
            v.wide[part, cols] = nt(v.trf[part, :], qkv_f[cols, :])

        tiles(640, 320, 512, 256, dh_fine)

        @pl.loop(0, 4)
        def _(i):
            part = aligned(i * 160, 160, 16)
            d = norm_back(v.wide[part, :], v.hf[part, :], v.sf[part, :])
            v.xf[part, :] = (d.astype(bf16).astype(f32) + v.yf[part, :].astype(f32)).astype(bf16)

        pack("fine_b", v.xf[...], got.fine_halo_t)
        copies = shift("fine_b")
        fine_pack_t = got.fine_pack_t
        finish(shift_out)
        out = nn(got.coarse_pack_t[...], recv_buf["coarse_b"][...]).astype(bf16)
        for r in range(6):
            coarse_ref[r] = out[16 * r : 16 * r + 6]
        finish(copies)
        writes = []
        fine_own_t = got.fine_own_t
        for j in range(4):
            part = pl.ds(j * 144, 144)
            here = (j * 160, min(j * 160 + 320, 640))
            d = nn(fine_own_t[:, : here[1] - here[0]], v.xf[here[0] : here[1], :])
            d += nn(fine_pack_t[part, :], recv_buf["fine_b"][...])
            tokens[part, :] = d.astype(bf16)
            writes.append(pltpu.make_async_copy(tokens.at[part], grad_ref.at[part], local_sem.at[len(ALL_LOADED) + 3 + j]))
            writes[-1].start()
        for write in writes:
            write.wait()
        for copy in pending:
            copy.wait_send()
        for name in ALL_LOADED:
            getattr(got, name)

    any_space = pl.BlockSpec(memory_space=pl.ANY)
    whole = pl.BlockSpec(memory_space=pltpu.VMEM)
    return pl.pallas_call(
        kernel,
        out_shape=(jax.ShapeDtypeStruct((576, 512), bf16), jax.ShapeDtypeStruct((6, 6, 2048), bf16)),
        in_specs=[any_space] * len(shapes),
        out_specs=(any_space, whole),
        scratch_shapes=[pltpu.VMEM(*shape) for group in (scratch, loaded, sends, receives) for shape in group.values()]
        + [pltpu.SemaphoreType.DMA((N_LOCAL,)), pltpu.SemaphoreType.DMA((N_REMOTE,)), pltpu.SemaphoreType.DMA((N_REMOTE,))],
        compiler_params=pltpu.CompilerParams(
            collective_id=0, has_side_effects=True, vmem_limit_bytes=66_584_576
        ),
    )


def shards(
    tokens, qkv_fine, out_fine, merge_fine, qkv_mid, out_mid, merge_mid, qkv_coarse, out_coarse, grad_fine, grad_mid, grad_coarse
):
    values = dict(
        tokens=tokens.reshape(576, 512),
        qkv_f=qkv_fine,
        out_f=out_fine,
        mrg_f=merge_fine,
        qkv_m=qkv_mid,
        out_m=out_mid,
        wm=merge_mid,
        wq=qkv_coarse,
        wo=out_coarse,
        g_fine=grad_fine.reshape(576, 512),
        g_mid=grad_mid,
        g_coarse=grad_coarse,
        bias=jnp.asarray(BIAS),
        biasc=jnp.asarray(BIASC),
    )
    for name, matrix in CONSTANTS.items():
        values[name] = jnp.asarray(matrix, bf16)
    shapes = {name: (value.shape, value.dtype) for name, value in values.items()}
    gradient, coarse = build(shapes)(*values.values())
    return gradient.reshape(24, 24, 512), coarse


def solution(mesh):
    placed = (
        P("lat", "lon", None),
        P(),
        P(),
        P(),
        P(),
        P(),
        P("lon", None),
        P(None, "lon"),
        P("lon", None),
        P("lat", "lon", None),
        P("lat", "lon", None),
        P("lat", "lon", None),
    )
    return jax.shard_map(
        shards,
        mesh=mesh,
        in_specs=placed,
        out_specs=(P("lat", "lon", None), P("lat", "lon", None)),
        check_vma=False,
    )
```

profile of v0, /device:TPU:1, one launch (start us, length us, event | category | flops | bytes accessed | tf_op | source)
XLA Modules:
  0.0 196.3 jit_solution(5344704052570655104)
XLA Ops:
  0.6 192.2 %shard_map.383 = (bf16[576,512]{1,0:T(8,128)(2,1)}, bf16[6,6,2048]{2,1,0:T(8,128)(2,1)}) custom-call(bf16[576,512]{1,0:T(8,128)(2,1)} %bitcast.3, bf16[512,1536]{1,0:T(8,128)(2,1)} %refs_1_.1, bf16[512,512]{1,0:T(8,128)(2,1)} %refs_2_.1, bf16[2048,1024]{1,0:T(8,128)(2,1)} %refs_3_.1, bf16[1024,3072]{1,0:T(8,128)(2,1)} %refs_4_.1, ...), custom_call_target="tpu_custom_call" | custom-call | tf_op jit(solution)/shard_map/pallas_call | solution.py:888
  192.8 1.9 copy.44
  194.7 1.6 copy.45
where the time goes:
time: 198 us; the launch traced here: 196 us
  Pallas kernels  192 us (97%)
  local copies, waits for them, and re-layouts  3.53 us (2%)
    pallas_call x1, Pallas kernels, shards(): gradient, coarse = build(shapes)(*values.values())  192 us

commit v1 on v0

--- a/solution.py
+++ b/solution.py
@@ -211,6 +211,7 @@
     @pl.loop(0, pairs * windows // unroll)
     def _(step):
         low, mlo, mhi = halves()
+        stores = []
         for u in range(unroll):
             item = step * unroll + u
             w, p = lax.div(item, pairs), lax.rem(item, pairs)
@@ -228,9 +229,11 @@
                 ds = wide * (dw - jnp.sum(wide * dw, axis=-1, keepdims=True)) * HD**-0.5
                 outs.append((wt, ds.astype(bf16)))
             (w0, ds0), (w1, ds1) = outs
-            tr[places[0]] = jnp.where(low, nn(ds0, k2), tn(ds0, q2)).astype(bf16)
-            tr[places[1]] = jnp.where(low, tn(w0, do), nn(ds1, k2)).astype(bf16)
-            tr[places[2]] = jnp.where(low, tn(ds1, q2), tn(w1, do)).astype(bf16)
+            stores.append((places[0], jnp.where(low, nn(ds0, k2), tn(ds0, q2)).astype(bf16)))
+            stores.append((places[1], jnp.where(low, tn(w0, do), nn(ds1, k2)).astype(bf16)))
+            stores.append((places[2], jnp.where(low, tn(ds1, q2), tn(w1, do)).astype(bf16)))
+        for place, value in stores:
+            tr[place] = value
 
 
 def tiles(rows, step, cols, width, body):
@@ -486,6 +489,10 @@
             v.hf[part, :] = h.astype(bf16)
             v.sf[part, :] = scale
 
+        for r in range(6):
+            v.gc[16 * r : 16 * r + 6, :] = got.g_coarse[r]
+        pack("gc", v.gc[...], got.coarse_pack)
+        shift_gc = shift("gc")
         start_loads(LOADED[2])
         for copy in own_loads:
             copy.start()
@@ -494,21 +501,7 @@
         project_qkv(v.hf, lambda p: qkv_f[:, aligned(p * 384, 384, 128)], v.trf, v.trrf, 640, 4, 320)
         first = lat == 0
         bias, out_f = got.bias, got.out_f
-        for part in range(2):
-            if part == 1:
-                relay_weights("wm", 0)
-                for r in range(6):
-                    v.gc[16 * r : 16 * r + 6, :] = got.g_coarse[r]
-                for r in range(12):
-                    v.gm[16 * r : 16 * r + 12, :] = got.g_mid[r]
-                pack("gc", v.gc[...], got.coarse_pack)
-                shift_gc = shift("gc")
-                pack("gf", got.g_fine[TOP:, :], got.fine_pack)
-                shift_gf = shift("gf")
-                pack("gm", v.gm[...], got.mid_pack)
-                shift_gm = shift("gm")
-                cross_weights("wq", 0)
-            attend(v.trf, v.trrf, v.psf, v.mixf, bias, 4, 8, WP, lambda w: jnp.where(first & (w < 2), 1, 0), 4, part, 2)
+        attend(v.trf, v.trrf, v.psf, v.mixf, bias, 4, 8, WP, lambda w: jnp.where(first & (w < 2), 1, 0), 4)
 
         def out_fine(part, cols):
             v.yf[part, cols] = (nn(v.mixf[part, :], out_f[:, cols]) + v.xf[part, cols].astype(f32)).astype(bf16)
@@ -553,15 +546,19 @@
             @pl.when(core != wide_group)
             def _():
                 across.start()
-                across.wait_send()
-
-            return source, dest, send, recv
+
+            return source, dest, send, recv, across
 
         def is_own(s):
             return (z == core * 2 + s // 2) & (core == s % 2)
 
         def from_group(handle):
-            source, dest, send, recv = handle
+            source, dest, send, recv, across = handle
+
+            @pl.when(core != wide_group)
+            def _():
+                across.wait_send()
+
             for s in range(4):
 
                 @pl.when(jnp.logical_not(is_own(s)))
@@ -607,30 +604,30 @@
             dest[z] = own
             return copies
 
+        finish(shift_gc)
+        v.ac[...] = nn(got.coarse_halo[...], recv_buf["gc"][...]).astype(bf16)
+        squeeze(v.ac[...], v.acs)
         received(shift_fold)
+        adjoint = to_group(v.acs, v.acr)
+        relay_weights("wm", 0)
+        cross_weights("wq", 0)
 
         quads = [placed(slice(k * 160, (k + 1) * 160), v.yf, "fold", fold_own, fold_halo) for k in range(4)]
         normed, scale = norm_split(quads)
         for k in range(4):
             v.ff[:, k * 512 : (k + 1) * 512] = normed[k].astype(bf16)
         v.sff[...] = scale
-        relay_weights("wq", 0)
-        cross_weights("wq", 1)
-        finish(shift_gf)
-        finish(shift_gc)
-        v.ac[...] = nn(got.coarse_halo[...], recv_buf["gc"][...]).astype(bf16)
-        squeeze(v.ac[...], v.acs)
-        adjoint = to_group(v.acs, v.acr)
-
-        @pl.loop(0, 4)
-        def _(i):
-            part = aligned(i * 160, 160, 16)
-            v.yf[part, :] = placed_fine(i, got.g_fine, "gf").astype(bf16)
-
         def merge_fine(part, cols):
             v.xm[part, cols] = nn(v.ff[part, :], mrg_f[:, cols]).astype(bf16)
 
         tiles(160, 160, 1024, 256, merge_fine)
+
+        for r in range(12):
+            v.gm[16 * r : 16 * r + 12, :] = got.g_mid[r]
+        pack("gm", v.gm[...], got.mid_pack)
+        shift_gm = shift("gm")
+        pack("gf", got.g_fine[TOP:, :], got.fine_pack)
+        shift_gf = shift("gf")
 
         qkv_m, out_m = got.qkv_m, got.out_m
         h, scale = norm_rows(v.xm[...].astype(f32))
@@ -639,8 +636,6 @@
         project_qkv(v.hm, lambda p: qkv_m[:, aligned(p * 384, 384, 128)], v.trm, v.trrm, 160, 8, 160)
         attend(v.trm, v.trrm, v.psm, v.mixm, bias, 8, 2, WP, lambda w: jnp.where(first & (w < 1), 1, 0), 4)
 
-        pass_weights("wm")
-
         def out_mid(part, cols):
             v.ym[part, cols] = (nn(v.mixm[part, :], out_m[:, cols]) + v.xm[part, cols].astype(f32)).astype(bf16)
 
@@ -648,13 +643,12 @@
 
         pack("foldc", v.ym[...], got.foldc_pack)
         shift_foldc = shift("foldc")
-        for copy in own_loads:
-            copy.wait()
-        weights_ready("wm")
         foldc_own, foldc_halo = got.foldc_own, got.foldc_halo
         received(shift_foldc)
-        relay_weights("wq", 1)
+        relay_weights("wq", 0)
+        cross_weights("wq", 1)
         cross_weights("wo", 0)
+        pass_weights("wm")
         folded = placed(slice(None), v.ym, "foldc", foldc_own, foldc_halo)
         quads = [folded[k * KP : (k + 1) * KP] for k in range(4)]
         normed, scale = norm_split(quads)
@@ -667,6 +661,9 @@
                 v.fcs[block % 4, :, (block // 4) * 512 : (block // 4 + 1) * 512] = h[:, j * 512 : (j + 1) * 512]
         copies = around(lambda k: v.fcs.at[turn(k)], v.fcr, v.fcs[z])
         finish(copies)
+        for copy in own_loads:
+            copy.wait()
+        weights_ready("wm")
         gathered = v.fcr[...].reshape(4 * KP, 1024)
 
         @pl.loop(0, 8)
@@ -680,8 +677,15 @@
         for k in range(4):
             squeeze(v.stage[k], v.pms.at[k])
         copies = around(lambda k: v.pms.at[turn(k)], v.pmr, v.pms[z])
+        relay_weights("wq", 1)
         relay_weights("wo", 0)
-        pass_weights("wq")
+        finish(shift_gf)
+
+        @pl.loop(0, 4)
+        def _(i):
+            part = aligned(i * 160, 160, 16)
+            v.yf[part, :] = placed_fine(i, got.g_fine, "gf").astype(bf16)
+
         finish(copies)
         x = total_of(v.pmr).astype(bf16)
         v.xc[...] = x
@@ -691,18 +695,19 @@
 
         squeeze(v.hc[...], v.hcs)
         forward = to_group(v.hcs, v.hcr)
+        pass_weights("wq")
+        pass_weights("wo")
         biasc = got.biasc
+        from_group(adjoint)
+        spread_all(v.acr)
+        weights_ready("wo")
+        for p in range(4):
+            v.dmixc[:, p * 128 : (p + 1) * 128] = nt(v.stage[...].reshape(4 * KP, 2048), v.wo[p]).astype(bf16)
         weights_ready("wq")
         from_group(forward)
         spread_all(v.hcr)
-        pass_weights("wo")
         project_qkv(v.stage.reshape(4 * KP, 2048), lambda p: v.wq[p], v.trc, v.trrc, 4 * KP, 4, 4 * KP)
         attend(v.trc, v.trrc, v.psc, v.mixc, biasc, 4, 2, 2 * KP, lambda w: jnp.where(first, 1, 0), 4)
-        from_group(adjoint)
-        weights_ready("wo")
-        spread_all(v.acr)
-        for p in range(4):
-            v.dmixc[:, p * 128 : (p + 1) * 128] = nt(v.stage[...].reshape(4 * KP, 2048), v.wo[p]).astype(bf16)
         attend_back(v.trc, v.trrc, v.psc, v.dmixc, 4, 2, 2 * KP, 4)
 
         @pl.loop(0, 8)
@@ -830,14 +835,15 @@
         out = nn(got.coarse_pack_t[...], recv_buf["coarse_b"][...]).astype(bf16)
         for r in range(6):
             coarse_ref[r] = out[16 * r : 16 * r + 6]
-        finish(copies)
         writes = []
         fine_own_t = got.fine_own_t
         for j in range(4):
+            here = (j * 160, min(j * 160 + 320, 640))
+            v.wide[pl.ds(j * 144, 144), :] = nn(fine_own_t[:, : here[1] - here[0]], v.xf[here[0] : here[1], :])
+        finish(copies)
+        for j in range(4):
             part = pl.ds(j * 144, 144)
-            here = (j * 160, min(j * 160 + 320, 640))
-            d = nn(fine_own_t[:, : here[1] - here[0]], v.xf[here[0] : here[1], :])
-            d += nn(fine_pack_t[part, :], recv_buf["fine_b"][...])
+            d = v.wide[part, :] + nn(fine_pack_t[part, :], recv_buf["fine_b"][...])
             tokens[part, :] = d.astype(bf16)
             writes.append(pltpu.make_async_copy(tokens.at[part], grad_ref.at[part], local_sem.at[len(ALL_LOADED) + 3 + j]))
             writes[-1].start()

time: 198 us -> 174 us (0.88)
  Pallas kernels: 192 us -> 170 us
    pallas_call x1, Pallas kernels: 192 us -> 170 us  [shards(): gradient, coarse = build(shapes)(*values.values())]
where the time goes in v1:
time: 174 us
  Pallas kernels  170 us (98%)
  local copies, waits for them, and re-layouts  3.53 us (2%)
    pallas_call x1, Pallas kernels, shards(): gradient, coarse = build(shapes)(*values.values())  170 us
    unnamed x2, local copies, waits for them, and re-layouts  3.53 us

profile of v1, /device:TPU:1, one launch (start us, length us, event | category | flops | bytes accessed | tf_op | source)
XLA Modules:
  0.0 173.8 jit_solution(16253254071283063999)
XLA Ops:
  0.6 169.6 %shard_map.383 = (bf16[576,512]{1,0:T(8,128)(2,1)}, bf16[6,6,2048]{2,1,0:T(8,128)(2,1)}) custom-call(bf16[576,512]{1,0:T(8,128)(2,1)} %bitcast.3, bf16[512,1536]{1,0:T(8,128)(2,1)} %refs_1_.1, bf16[512,512]{1,0:T(8,128)(2,1)} %refs_2_.1, bf16[2048,1024]{1,0:T(8,128)(2,1)} %refs_3_.1, bf16[1024,3072]{1,0:T(8,128)(2,1)} %refs_4_.1, ...), custom_call_target="tpu_custom_call" | custom-call | tf_op jit(solution)/shard_map/pallas_call | solution.py:894
  170.3 1.9 %copy.44 = bf16[24,24,512]{2,1,0:T(8,128)(2,1)} copy(bf16[24,24,512]{2,1,0:T(8,128)(2,1)} %bitcast.5) | data formatting | bytes 1179648
  172.2 1.6 copy.45

commit v2 on v1

--- a/solution.py
+++ b/solution.py
@@ -168,7 +168,7 @@
     def _(i):
         part = aligned(i * step, step, 16)
 
-        @pl.loop(0, pairs)
+        @pl.loop(0, pairs, unroll=2)
         def _(p):
             wide = nn(h[part, :], weight(p))
             tr[part, aligned(p * 384, 384, 128)] = wide.astype(bf16)
@@ -191,6 +191,7 @@
     @pl.loop(part * steps, (part + 1) * steps)
     def _(step):
         low, mlo, mhi = halves()
+        stores = []
         for u in range(unroll):
             item = step * unroll + u
             w, p = lax.div(item, pairs), lax.rem(item, pairs)
@@ -202,9 +203,11 @@
             scores = nt(q2, k2) + bias[split(w)]
             e = jnp.exp(scores - jnp.max(scores, axis=-1, keepdims=True))
             weights = (e / jnp.sum(e, axis=-1, keepdims=True)).astype(bf16)
+            mixed = jnp.where(low, nn(weights[:wp], b), nn(weights[wp:], c))
+            stores.append((item, weights, (part, aligned(p * 128, 128, 128)), mixed.astype(bf16)))
+        for item, weights, place, mixed in stores:
             ps[item] = weights
-            mixed = jnp.where(low, nn(weights[:wp], b), nn(weights[wp:], c))
-            mix[part, aligned(p * 128, 128, 128)] = mixed.astype(bf16)
+            mix[place] = mixed
 
 
 def attend_back(tr, trr, ps, dmix, pairs, windows, wp, unroll):
@@ -241,7 +244,7 @@
     def _(i):
         part = aligned(i * step, step, 16)
 
-        @pl.loop(0, cols // width)
+        @pl.loop(0, cols // width, unroll=2)
         def _(j):
             body(part, aligned(j * width, width, 128))
 
@@ -256,13 +259,12 @@
     fc=((KP, 4096), bf16), sfc=((KP, 1), f32), fcs=((4, KP, 1024), bf16), fcr=((4, KP, 1024), bf16),
     pms=((4, 144, 512), bf16), pmr=((4, 144, 512), bf16), dmo=((144, 512), bf16), dms=((4, 144, 512), bf16), stage=((4, KP, 2048), bf16),
     dsr=((4, KP, 1024), bf16), dfc=((4 * KP, 1024), bf16),
-    gm=((192, 1024), bf16), gc=((96, 2048), bf16),
+    gm=((192, 1024), bf16),
     xc=((KP, 2048), bf16), hc=((KP, 2048), bf16), sc=((KP, 1), f32), hcs=((144, 512), bf16), hcr=((4, 144, 512), bf16),
     ac=((KP, 2048), bf16), acs=((144, 512), bf16), acr=((4, 144, 512), bf16),
     trc=((4 * KP, 1536), bf16), trrc=((4 * KP, 1024), bf16), psc=((8, 4 * KP, 2 * KP), bf16),
     mixc=((4 * KP, 512), bf16), dmixc=((4 * KP, 512), bf16),
     dhs=((4, 144, 512), bf16), dhr=((4, 144, 512), bf16), pos=((4, 144, 512), bf16), por=((4, 144, 512), bf16),
-    yc=((KP, 2048), bf16),
     wm=((4, 256, 2048), bf16), wq=((4, 2048, 384), bf16), wo=((4, 128, 2048), bf16),
 )
 EXCHANGES = dict(
@@ -466,7 +468,6 @@
         tokens[0:TOP, :] = jnp.zeros((TOP, 512), bf16)
         vm["g_fine"][0:TOP, :] = jnp.zeros((TOP, 512), bf16)
         v.gm[...] = jnp.zeros_like(v.gm)
-        v.gc[...] = jnp.zeros_like(v.gc)
         fine_own, fine_halo, qkv_f = got.fine_own, got.fine_halo, got.qkv_f
 
         def placed(part, source, name, own, halo):
@@ -480,7 +481,7 @@
         received(shift_tok)
         cross_weights("wm", 0)
 
-        @pl.loop(0, 4)
+        @pl.loop(0, 4, unroll=2)
         def _(i):
             part = aligned(i * 160, 160, 16)
             x = placed_fine(i, tokens, "tok")
@@ -490,8 +491,11 @@
             v.sf[part, :] = scale
 
         for r in range(6):
-            v.gc[16 * r : 16 * r + 6, :] = got.g_coarse[r]
-        pack("gc", v.gc[...], got.coarse_pack)
+            for k in range(2):
+                v.gm[96 * k + 16 * r : 96 * k + 16 * r + 6, :] = got.g_coarse[r, :, k * 1024 : (k + 1) * 1024]
+        for k in range(2):
+            packed = nn(got.coarse_pack[...], v.gm[96 * k : 96 * (k + 1), :])
+            sender("gc")[:, k * 1024 : (k + 1) * 1024] = packed.astype(bf16)
         shift_gc = shift("gc")
         start_loads(LOADED[2])
         for copy in own_loads:
@@ -501,7 +505,7 @@
         project_qkv(v.hf, lambda p: qkv_f[:, aligned(p * 384, 384, 128)], v.trf, v.trrf, 640, 4, 320)
         first = lat == 0
         bias, out_f = got.bias, got.out_f
-        attend(v.trf, v.trrf, v.psf, v.mixf, bias, 4, 8, WP, lambda w: jnp.where(first & (w < 2), 1, 0), 4)
+        attend(v.trf, v.trrf, v.psf, v.mixf, bias, 4, 8, WP, lambda w: jnp.where(first & (w < 2), 1, 0), 8)
 
         def out_fine(part, cols):
             v.yf[part, cols] = (nn(v.mixf[part, :], out_f[:, cols]) + v.xf[part, cols].astype(f32)).astype(bf16)
@@ -634,7 +638,7 @@
         v.hm[...] = h.astype(bf16)
         v.sm[...] = scale
         project_qkv(v.hm, lambda p: qkv_m[:, aligned(p * 384, 384, 128)], v.trm, v.trrm, 160, 8, 160)
-        attend(v.trm, v.trrm, v.psm, v.mixm, bias, 8, 2, WP, lambda w: jnp.where(first & (w < 1), 1, 0), 4)
+        attend(v.trm, v.trrm, v.psm, v.mixm, bias, 8, 2, WP, lambda w: jnp.where(first & (w < 1), 1, 0), 8)
 
         def out_mid(part, cols):
             v.ym[part, cols] = (nn(v.mixm[part, :], out_m[:, cols]) + v.xm[part, cols].astype(f32)).astype(bf16)
@@ -666,7 +670,7 @@
         weights_ready("wm")
         gathered = v.fcr[...].reshape(4 * KP, 1024)
 
-        @pl.loop(0, 8)
+        @pl.loop(0, 8, unroll=4)
         def _(j):
             cols = aligned(j * 256, 256, 128)
             total = nn(gathered[:, 0:256], v.wm[0, :, cols])
@@ -681,7 +685,7 @@
         relay_weights("wo", 0)
         finish(shift_gf)
 
-        @pl.loop(0, 4)
+        @pl.loop(0, 4, unroll=2)
         def _(i):
             part = aligned(i * 160, 160, 16)
             v.yf[part, :] = placed_fine(i, got.g_fine, "gf").astype(bf16)
@@ -707,10 +711,10 @@
         from_group(forward)
         spread_all(v.hcr)
         project_qkv(v.stage.reshape(4 * KP, 2048), lambda p: v.wq[p], v.trc, v.trrc, 4 * KP, 4, 4 * KP)
-        attend(v.trc, v.trrc, v.psc, v.mixc, biasc, 4, 2, 2 * KP, lambda w: jnp.where(first, 1, 0), 4)
-        attend_back(v.trc, v.trrc, v.psc, v.dmixc, 4, 2, 2 * KP, 4)
-
-        @pl.loop(0, 8)
+        attend(v.trc, v.trrc, v.psc, v.mixc, biasc, 4, 2, 2 * KP, lambda w: jnp.where(first, 1, 0), 8)
+        attend_back(v.trc, v.trrc, v.psc, v.dmixc, 4, 2, 2 * KP, 8)
+
+        @pl.loop(0, 8, unroll=4)
         def _(j):
             rows = aligned(j * 256, 256, 128)
             total = nt(v.trc[:, 0:384], v.wq[0, rows, :])
@@ -722,7 +726,7 @@
             squeeze(v.stage[k], v.dhs.at[k])
         backward = to_owners(v.dhs, v.dhr)
 
-        @pl.loop(0, 8)
+        @pl.loop(0, 8, unroll=4)
         def _(j):
             cols = aligned(j * 256, 256, 128)
             total = nn(v.mixc[:, 0:128], v.wo[0, :, cols])
@@ -771,16 +775,15 @@
             v.mixm[part, cols] = nt(v.ym[part, :], out_m[cols, :]).astype(bf16)
 
         tiles(160, 160, 1024, 256, dmix_mid)
-        attend_back(v.trm, v.trrm, v.psm, v.mixm, 8, 2, WP, 4)
+        attend_back(v.trm, v.trrm, v.psm, v.mixm, 8, 2, WP, 8)
 
         from_members(outward)
         total = total_of(v.por)
-        v.yc[...] = (v.xc[...].astype(f32) + total).astype(bf16)
-        pack("coarse_b", v.yc[...], got.coarse_halo_t)
+        pack("coarse_b", (v.xc[...].astype(f32) + total).astype(bf16), got.coarse_halo_t)
         shift_out = shift("coarse_b")
 
         def to_wide(left, weight, blocks):
-            @pl.loop(0, 2 * blocks)
+            @pl.loop(0, 2 * blocks, unroll=4)
             def _(j):
                 v.wide[aligned(lax.div(j, 2) * 160, 160, 16), aligned(lax.rem(j, 2) * 256, 256, 128)] = nt(
                     left[...], weight[aligned(j * 256, 256, 128), :]
@@ -805,7 +808,7 @@
         fold_pack_t = got.fold_pack_t
         finish(copies)
 
-        @pl.loop(0, 5)
+        @pl.loop(0, 5, unroll=5)
         def _(i):
             part = aligned(i * 128, 128, 128)
             d = tn(fold_own[:, part], v.mixf[...]) + nn(fold_pack_t[part, :], recv_buf["fold_b"][...])
@@ -815,14 +818,14 @@
             v.mixf[part, cols] = nt(v.yf[part, :], out_f[cols, :]).astype(bf16)
 
         tiles(640, 320, 512, 256, dmix_fine)
-        attend_back(v.trf, v.trrf, v.psf, v.mixf, 4, 8, WP, 4)
+        attend_back(v.trf, v.trrf, v.psf, v.mixf, 4, 8, WP, 8)
 
         def dh_fine(part, cols):
             v.wide[part, cols] = nt(v.trf[part, :], qkv_f[cols, :])
 
         tiles(640, 320, 512, 256, dh_fine)
 
-        @pl.loop(0, 4)
+        @pl.loop(0, 4, unroll=2)
         def _(i):
             part = aligned(i * 160, 160, 16)
             d = norm_back(v.wide[part, :], v.hf[part, :], v.sf[part, :])

time: 174 us -> 164 us (0.943)
  Pallas kernels: 170 us -> 160 us
    pallas_call x1, Pallas kernels: 170 us -> 160 us  [shards(): gradient, coarse = build(shapes)(*values.values())]
where the time goes in v2:
time: 164 us
  Pallas kernels  160 us (98%)
  local copies, waits for them, and re-layouts  3.53 us (2%)
    pallas_call x1, Pallas kernels, shards(): gradient, coarse = build(shapes)(*values.values())  160 us
    unnamed x2, local copies, waits for them, and re-layouts  3.53 us

profile of v2, /device:TPU:1, one launch (start us, length us, event | category | flops | bytes accessed | tf_op | source)
XLA Modules:
  0.0 164.1 jit_solution(11169101395217273612)
XLA Ops:
  0.6 159.9 %shard_map.383 = (bf16[576,512]{1,0:T(8,128)(2,1)}, bf16[6,6,2048]{2,1,0:T(8,128)(2,1)}) custom-call(bf16[576,512]{1,0:T(8,128)(2,1)} %bitcast.3, bf16[512,1536]{1,0:T(8,128)(2,1)} %refs_1_.1, bf16[512,512]{1,0:T(8,128)(2,1)} %refs_2_.1, bf16[2048,1024]{1,0:T(8,128)(2,1)} %refs_3_.1, bf16[1024,3072]{1,0:T(8,128)(2,1)} %refs_4_.1, ...), custom_call_target="tpu_custom_call" | custom-call | tf_op jit(solution)/shard_map/pallas_call | solution.py:897
  160.5 1.9 %copy.44 = bf16[24,24,512]{2,1,0:T(8,128)(2,1)} copy(bf16[24,24,512]{2,1,0:T(8,128)(2,1)} %bitcast.5) | data formatting | bytes 1179648
  162.4 1.6 copy.45

commit v3 on v2

--- a/solution.py
+++ b/solution.py
@@ -244,7 +244,7 @@
     def _(i):
         part = aligned(i * step, step, 16)
 
-        @pl.loop(0, cols // width, unroll=2)
+        @pl.loop(0, cols // width, unroll=min(4, cols // width))
         def _(j):
             body(part, aligned(j * width, width, 128))
 
@@ -608,6 +608,13 @@
             dest[z] = own
             return copies
 
+        for r in range(12):
+            v.gm[16 * r : 16 * r + 12, :] = got.g_mid[r]
+        pack("gm", v.gm[...], got.mid_pack)
+        shift_gm = shift("gm")
+        pack("gf", got.g_fine[TOP:, :], got.fine_pack)
+        shift_gf = shift("gf")
+
         finish(shift_gc)
         v.ac[...] = nn(got.coarse_halo[...], recv_buf["gc"][...]).astype(bf16)
         squeeze(v.ac[...], v.acs)
@@ -625,13 +632,6 @@
             v.xm[part, cols] = nn(v.ff[part, :], mrg_f[:, cols]).astype(bf16)
 
         tiles(160, 160, 1024, 256, merge_fine)
-
-        for r in range(12):
-            v.gm[16 * r : 16 * r + 12, :] = got.g_mid[r]
-        pack("gm", v.gm[...], got.mid_pack)
-        shift_gm = shift("gm")
-        pack("gf", got.g_fine[TOP:, :], got.fine_pack)
-        shift_gf = shift("gf")
 
         qkv_m, out_m = got.qkv_m, got.out_m
         h, scale = norm_rows(v.xm[...].astype(f32))
@@ -777,11 +777,6 @@
         tiles(160, 160, 1024, 256, dmix_mid)
         attend_back(v.trm, v.trrm, v.psm, v.mixm, 8, 2, WP, 8)
 
-        from_members(outward)
-        total = total_of(v.por)
-        pack("coarse_b", (v.xc[...].astype(f32) + total).astype(bf16), got.coarse_halo_t)
-        shift_out = shift("coarse_b")
-
         def to_wide(left, weight, blocks):
             @pl.loop(0, 2 * blocks, unroll=4)
             def _(j):
@@ -805,6 +800,12 @@
         sent(shift_fold)
         pack("fold_b", v.mixf[...], got.fold_halo_t)
         copies = shift("fold_b")
+
+        from_members(outward)
+        total = total_of(v.por)
+        pack("coarse_b", (v.xc[...].astype(f32) + total).astype(bf16), got.coarse_halo_t)
+        shift_out = shift("coarse_b")
+
         fold_pack_t = got.fold_pack_t
         finish(copies)
 

time: 164 us -> 164 us (level)
  no operation moved by 1% of the time
where the time goes in v3:
time: 164 us
  Pallas kernels  160 us (98%)
  local copies, waits for them, and re-layouts  3.53 us (2%)
    pallas_call x1, Pallas kernels, shards(): gradient, coarse = build(shapes)(*values.values())  160 us
    unnamed x2, local copies, waits for them, and re-layouts  3.53 us

profile of v3, /device:TPU:1, one launch (start us, length us, event | category | flops | bytes accessed | tf_op | source)
XLA Modules:
  0.0 164.2 jit_solution(7204033985534161097)
XLA Ops:
  0.6 160.0 %shard_map.383 = (bf16[576,512]{1,0:T(8,128)(2,1)}, bf16[6,6,2048]{2,1,0:T(8,128)(2,1)}) custom-call(bf16[576,512]{1,0:T(8,128)(2,1)} %bitcast.3, bf16[512,1536]{1,0:T(8,128)(2,1)} %refs_1_.1, bf16[512,512]{1,0:T(8,128)(2,1)} %refs_2_.1, bf16[2048,1024]{1,0:T(8,128)(2,1)} %refs_3_.1, bf16[1024,3072]{1,0:T(8,128)(2,1)} %refs_4_.1, ...), custom_call_target="tpu_custom_call" | custom-call | tf_op jit(solution)/shard_map/pallas_call | solution.py:898
  160.7 1.9 %copy.44 = bf16[24,24,512]{2,1,0:T(8,128)(2,1)} copy(bf16[24,24,512]{2,1,0:T(8,128)(2,1)} %bitcast.5) | data formatting | bytes 1179648
  162.6 1.6 copy.45

commit v4 on v3

--- a/solution.py
+++ b/solution.py
@@ -361,7 +361,6 @@
             pl.semaphore_signal(barrier, inc=1, device_id=near(0, -1), device_id_type=MESH)
 
         edge = jnp.where((place == 7) | (place == 0), 1, 0)
-        pl.semaphore_wait(barrier, len(others) + edge)
 
         counter = [0]
 
@@ -463,6 +462,7 @@
 
         tokens = got.tokens
         pack("tok", tokens[TOP:, :], got.fine_pack)
+        pl.semaphore_wait(barrier, len(others) + edge)
         shift_tok = shift("tok")
         start_loads(LOADED[1])
         tokens[0:TOP, :] = jnp.zeros((TOP, 512), bf16)
@@ -569,9 +569,10 @@
                 def _(s=s):
                     remote(source, dest.at[s], send, recv + s, sibling).wait_recv()
 
-        def to_owners(source, dest):
+        def to_owners(source, dest, prepare):
             send, recv = sems(4), sems(4)
             for s in range(4):
+                prepare(s)
                 copy = remote(source.at[s], dest.at[z], send + s, recv + z, at(y, core * 2 + s // 2, s % 2))
 
                 @pl.when(is_own(s))
@@ -605,7 +606,7 @@
                 copy = remote(pick(k), dest.at[z], base + k, base + k, at(y, turn(k), core))
                 copy.start()
                 copies.append(copy)
-            dest[z] = own
+            dest[z] = own()
             return copies
 
         for r in range(12):
@@ -663,7 +664,7 @@
             for j in range(2):
                 block = 2 * k + j
                 v.fcs[block % 4, :, (block // 4) * 512 : (block // 4 + 1) * 512] = h[:, j * 512 : (j + 1) * 512]
-        copies = around(lambda k: v.fcs.at[turn(k)], v.fcr, v.fcs[z])
+        copies = around(lambda k: v.fcs.at[turn(k)], v.fcr, lambda: v.fcs[z])
         finish(copies)
         for copy in own_loads:
             copy.wait()
@@ -678,9 +679,12 @@
                 total += nn(gathered[:, s * 256 : (s + 1) * 256], v.wm[s, :, cols])
             v.stage[:, :, cols] = total.astype(bf16).reshape(4, KP, 256)
 
-        for k in range(4):
-            squeeze(v.stage[k], v.pms.at[k])
-        copies = around(lambda k: v.pms.at[turn(k)], v.pmr, v.pms[z])
+        def merged_block(k):
+            block = v.pms.at[turn(k)]
+            squeeze(v.stage[turn(k)], block)
+            return block
+
+        copies = around(merged_block, v.pmr, lambda: merged_block(0)[...])
         relay_weights("wq", 1)
         relay_weights("wo", 0)
         finish(shift_gf)
@@ -722,9 +726,7 @@
                 total += nt(v.trc[:, s * 384 : (s + 1) * 384], v.wq[s, rows, :])
             v.stage[:, :, rows] = total.astype(bf16).reshape(4, KP, 256)
 
-        for k in range(4):
-            squeeze(v.stage[k], v.dhs.at[k])
-        backward = to_owners(v.dhs, v.dhr)
+        backward = to_owners(v.dhs, v.dhr, lambda s: squeeze(v.stage[s], v.dhs.at[s]))
 
         @pl.loop(0, 8, unroll=4)
         def _(j):
@@ -742,15 +744,15 @@
         d = (d.astype(bf16).astype(f32) + v.ac[...].astype(f32)).astype(bf16)
         squeeze(d, v.dmo)
 
-        copies = around(lambda k: v.dmo, v.dms, v.dmo[...])
+        copies = around(lambda k: v.dmo, v.dms, lambda: v.dmo[...])
         finish(copies)
         spread_all(v.dms)
         gathered_d = v.stage[...].reshape(4 * KP, 2048)
         for s in range(4):
             block = nt(gathered_d, v.wm[s]).astype(bf16)
             v.fcs[:, :, s * 256 : (s + 1) * 256] = block.reshape(4, KP, 256)
-        copies = around(lambda k: v.fcs.at[turn(k)], v.dsr, v.fcs[z])
-        outward = to_owners(v.pos, v.por)
+        copies = around(lambda k: v.fcs.at[turn(k)], v.dsr, lambda: v.fcs[z])
+        outward = to_owners(v.pos, v.por, lambda s: None)
         finish(copies)
 
         ds = []

time: 164 us -> 165 us (level)
  no operation moved by 1% of the time
where the time goes in v4:
time: 165 us; the launch traced here: 164 us
  Pallas kernels  160 us (97%)
  local copies, waits for them, and re-layouts  3.53 us (2%)
    pallas_call x1, Pallas kernels, shards(): gradient, coarse = build(shapes)(*values.values())  160 us
    unnamed x2, local copies, waits for them, and re-layouts  3.53 us

profile of v4, /device:TPU:1, one launch (start us, length us, event | category | flops | bytes accessed | tf_op | source)
XLA Modules:
  0.0 164.3 jit_solution(4056232100520632953)
XLA Ops:
  0.6 160.2 %shard_map.383 = (bf16[576,512]{1,0:T(8,128)(2,1)}, bf16[6,6,2048]{2,1,0:T(8,128)(2,1)}) custom-call(bf16[576,512]{1,0:T(8,128)(2,1)} %bitcast.3, bf16[512,1536]{1,0:T(8,128)(2,1)} %refs_1_.1, bf16[512,512]{1,0:T(8,128)(2,1)} %refs_2_.1, bf16[2048,1024]{1,0:T(8,128)(2,1)} %refs_3_.1, bf16[1024,3072]{1,0:T(8,128)(2,1)} %refs_4_.1, ...), custom_call_target="tpu_custom_call" | custom-call | tf_op jit(solution)/shard_map/pallas_call | solution.py:900
  160.8 1.9 %copy.44 = bf16[24,24,512]{2,1,0:T(8,128)(2,1)} copy(bf16[24,24,512]{2,1,0:T(8,128)(2,1)} %bitcast.5) | data formatting | bytes 1179648
  162.7 1.6 copy.45

commit v5 on v4

--- a/solution.py
+++ b/solution.py
@@ -616,13 +616,13 @@
         pack("gf", got.g_fine[TOP:, :], got.fine_pack)
         shift_gf = shift("gf")
 
+        relay_weights("wm", 0)
+        cross_weights("wq", 0)
         finish(shift_gc)
         v.ac[...] = nn(got.coarse_halo[...], recv_buf["gc"][...]).astype(bf16)
         squeeze(v.ac[...], v.acs)
         received(shift_fold)
         adjoint = to_group(v.acs, v.acr)
-        relay_weights("wm", 0)
-        cross_weights("wq", 0)
 
         quads = [placed(slice(k * 160, (k + 1) * 160), v.yf, "fold", fold_own, fold_halo) for k in range(4)]
         normed, scale = norm_split(quads)
@@ -649,11 +649,11 @@
         pack("foldc", v.ym[...], got.foldc_pack)
         shift_foldc = shift("foldc")
         foldc_own, foldc_halo = got.foldc_own, got.foldc_halo
-        received(shift_foldc)
         relay_weights("wq", 0)
         cross_weights("wq", 1)
         cross_weights("wo", 0)
         pass_weights("wm")
+        received(shift_foldc)
         folded = placed(slice(None), v.ym, "foldc", foldc_own, foldc_halo)
         quads = [folded[k * KP : (k + 1) * KP] for k in range(4)]
         normed, scale = norm_split(quads)

time: 165 us -> 168 us (1.018)
  Pallas kernels: 160 us -> 164 us
    pallas_call x1, Pallas kernels: 160 us -> 164 us  [shards(): gradient, coarse = build(shapes)(*values.values())]
where the time goes in v5:
time: 168 us
  Pallas kernels  164 us (98%)
  local copies, waits for them, and re-layouts  3.53 us (2%)
    pallas_call x1, Pallas kernels, shards(): gradient, coarse = build(shapes)(*values.values())  164 us
    unnamed x2, local copies, waits for them, and re-layouts  3.53 us

profile of v5, /device:TPU:1, one launch (start us, length us, event | category | flops | bytes accessed | tf_op | source)
XLA Modules:
  0.0 168.2 jit_solution(2356295204722948398)
XLA Ops:
  0.6 164.0 %shard_map.383 = (bf16[576,512]{1,0:T(8,128)(2,1)}, bf16[6,6,2048]{2,1,0:T(8,128)(2,1)}) custom-call(bf16[576,512]{1,0:T(8,128)(2,1)} %bitcast.3, bf16[512,1536]{1,0:T(8,128)(2,1)} %refs_1_.1, bf16[512,512]{1,0:T(8,128)(2,1)} %refs_2_.1, bf16[2048,1024]{1,0:T(8,128)(2,1)} %refs_3_.1, bf16[1024,3072]{1,0:T(8,128)(2,1)} %refs_4_.1, ...), custom_call_target="tpu_custom_call" | custom-call | tf_op jit(solution)/shard_map/pallas_call | solution.py:900
  164.6 1.9 %copy.44 = bf16[24,24,512]{2,1,0:T(8,128)(2,1)} copy(bf16[24,24,512]{2,1,0:T(8,128)(2,1)} %bitcast.5) | data formatting | bytes 1179648
  166.5 1.6 copy.45
